TPU v7x, 512 devices: a whole 4x8x8 slice. The times are simulated.
512 devices in a mesh: span: 64 (over x, z, core), wall: 8 (over y).
Axes of the slice: x: 4, y: 8, z: 8, core: 2. Of those that a mesh axis runs over, the one named last changes fastest.
Arguments:
- velocity: float32 [3, 2, 1536, 8192], P(None, None, 'wall', 'span'), may hold values from -6 to 6
- wave_x: float32 [2], replicated, may hold values from 0.01 to 0.1
Outputs:
- pressure: float32 [2, 1536, 8192], P(None, 'wall', 'span')
All inputs are finite; a program needn't handle non-finite values.
Results may differ from a plain program's by a relative error of at most 0.0023.
Values sent between devices are 32-bit elements; how exact they have to be, the bound alone decides.
No kernel may reach another device: no remote copies, remote signals or barrier semaphores. Data moves between devices by JAX's collectives and lax.ppermute only.
A program may use at most 64 MiB of HBM per device.

v0:
```python
import jax
import jax.numpy as jnp
import numpy as np
from jax import lax
from jax.experimental import pallas as pl
from jax.experimental.pallas import tpu as pltpu
from jax.sharding import PartitionSpec as P

F32 = jnp.float32
EXACT = lax.Precision.HIGHEST
NY, NZ = 1536, 8192
WALLS, STRIPS = 8, 64
ROWS, COLS = NY // WALLS, NZ // STRIPS
HALF = ROWS // 2


def sine_table(n):
    i = np.arange(1, n + 1)
    return np.sqrt(2 / (n + 1)) * np.sin(np.pi * np.outer(i, i) / (n + 1)), 4 * np.sin(np.pi * i / (2 * (n + 1))) ** 2


def tables():
    sine_y, mu_box = sine_table(ROWS)
    sine_z, lam = sine_table(COLS)
    sine_wide = np.zeros((ROWS, 256))
    sine_wide[:, :ROWS] = sine_y
    ends_y = np.zeros((8, ROWS))
    ends_y[0], ends_y[1] = sine_y[0], sine_y[-1]
    ends_z = np.zeros((8, COLS))
    ends_z[0], ends_z[1] = sine_z[0], sine_z[-1]
    edge_w = np.zeros((8, COLS))
    edge_w[0, 0], edge_w[1, -1] = -0.5, 0.5
    ends_tile = np.zeros((8, COLS))
    ends_tile[4] = ends_tile[6] = sine_z[0]
    ends_tile[5] = ends_tile[7] = sine_z[-1]
    r = np.arange(ROWS)
    wall = np.arange(WALLS)
    cosine = np.zeros((WALLS, 2 * ROWS, ROWS))
    fold = np.zeros((WALLS, 16, 64))
    spread = np.zeros((WALLS, 64, 16))
    ghost = np.zeros((WALLS, 64, ROWS))
    mu_col = np.zeros((WALLS, ROWS, COLS))
    mu_lane = np.zeros((WALLS, 24, COLS))
    for c in range(WALLS):
        mode = (c + 8 * np.arange(2)[:, None] + 16 * np.arange(HALF)[None, :]).reshape(-1)
        norm = np.where(mode == 0, np.sqrt(1 / NY), np.sqrt(2 / NY))
        angle = np.pi * np.outer(2 * r + 1, mode) / (2 * NY)
        cosine[c, :ROWS] = norm * np.cos(angle)
        cosine[c, ROWS:] = norm * np.sin(angle)
        for par in range(2):
            turn = np.pi * (c + 8 * par) * wall / 8
            for line in range(4):
                for w in range(WALLS):
                    for s in (line, line + 4):
                        fold[c, 4 * par + line, 8 * w + s] = np.cos(turn[w])
                        fold[c, 8 + 4 * par + line, 8 * w + s] = -np.sin(turn[w])
                    spread[c, 8 * w + line, 4 * par + line] = np.cos(turn[w])
                    spread[c, 8 * w + line, 8 + 4 * par + line] = -np.sin(turn[w])
        for w in range(WALLS):
            for g, y in enumerate((ROWS * w - 1, ROWS * (w + 1))):
                row = norm * np.cos(np.pi * mode * (2 * y + 1) / (2 * NY))
                ghost[c, 8 * w + 4 + g] = ghost[c, 8 * w + 6 + g] = row
        mu = 4 * np.sin(np.pi * mode / (2 * NY)) ** 2
        mu_col[c] = mu[:, None]
        six = np.stack([mu[:128]] * 4 + [np.concatenate([mu[128:], mu[128:]])] * 2)
        mu_lane[c] = np.concatenate([six] * 4)
    names = dict(
        sine_y=sine_y, sine_z=sine_z, sine_wide=sine_wide, ends_y=ends_y, ends_z=ends_z, edge_w=edge_w,
        ends_tile=ends_tile, both=mu_box[:, None] + lam[None, :], lam_col=np.repeat(lam[:, None], COLS, 1),
        lam_row=np.repeat(lam[None, :], 8, 0), cosine=cosine, fold=fold.reshape(-1, 64),
        spread=spread.reshape(-1, 16), ghost=ghost, mu_col=mu_col, mu_lane=mu_lane.reshape(-1, COLS),
    )
    return {key: np.asarray(value, np.float32) for key, value in names.items()}


def dot(a, b, dims=((1,), (0,))):
    return lax.dot_general(a, b, (dims, ((), ())), precision=EXACT, preferred_element_type=F32)


def ids(shape, dim):
    return lax.broadcasted_iota(jnp.int32, shape, dim)


def box_kernel(wave_ref, vel_ref, both_ref, sine_y_ref, sine_z_ref, wide_ref, ends_y_ref, ends_z_ref, edge_ref, out_ref, freq_ref):
    shape = (ROWS, COLS)
    row, lane = ids(shape, 0), ids(shape, 1)
    wall = lax.axis_index("wall")
    low = jnp.where(wall > 0, -0.5, 0.0)
    high = jnp.where(wall < WALLS - 1, 0.5, 0.0)
    sine_y, sine_z = sine_y_ref[...], sine_z_ref[...]
    edges, firsts, lasts = [], [], []
    for plane in range(2):
        u, v, w = (vel_ref[c, plane] for c in range(3))
        above = jnp.where(row == ROWS - 1, 0.0, pltpu.roll(v, ROWS - 1, 0))
        below = jnp.where(row == 0, 0.0, pltpu.roll(v, 1, 0))
        after = jnp.where(lane == COLS - 1, 0.0, pltpu.roll(w, COLS - 1, 1))
        before = jnp.where(lane == 0, 0.0, pltpu.roll(w, 1, 1))
        wave = wave_ref[plane]
        source = wave * u + 0.5 * ((above - below) + (after - before))
        freq = dot(dot(sine_y, source), sine_z)
        freq_ref[ROWS * plane : ROWS * (plane + 1), :] = freq
        inside = -freq / (wave * wave + both_ref[...])
        edge = dot(dot(ends_z_ref[...], inside, ((1,), (1,))), wide_ref[...])
        halo = dot(edge_ref[...], w, ((1,), (1,)))
        edge = edge + jnp.concatenate([halo, jnp.zeros((8, 256 - ROWS), F32)], 1)
        edges.append(edge[0:2])
        ends = dot(ends_y_ref[...], inside)
        rims = jnp.concatenate([low * v[0:1], high * v[ROWS - 1 :], jnp.zeros((6, COLS), F32)], 0)
        ends = ends + dot(rims, sine_z)
        firsts += [ends[0:1]] * 2
        lasts += [ends[1:2]] * 2
    tile = jnp.concatenate(edges + [jnp.concatenate([jnp.concatenate(firsts, 0), jnp.concatenate(lasts, 0)], 1)], 0)
    for w in range(WALLS):
        out_ref[8 * w : 8 * w + 8, :] = tile


def decay(shift):
    root = jnp.sqrt(shift * (shift + 4.0))
    delta = (shift + root) / (2.0 + shift + root)
    return 1.0 - delta, delta * (2.0 - delta), -jnp.log1p(-delta)


def factor_kernel(
    wave_ref, both_ref, lam_col_ref, lam_row_ref, mu_lane_ref, mu_col_ref, cosine_ref,
    solve_ref, reach_ref, chain_ref, cauchy_ref, left_ref, right_ref, mine_ref, mu_ref, sems,
):
    strip, wall = lax.axis_index("span"), lax.axis_index("wall")
    copies = [
        pltpu.make_async_copy(cosine_ref.at[wall], mine_ref, sems.at[0]),
        pltpu.make_async_copy(mu_col_ref.at[wall], mu_ref, sems.at[1]),
    ]
    for copy in copies:
        copy.start()
    waves = [wave_ref[p] * wave_ref[p] for p in range(2)]
    cell = ids((COLS, 256), 1)
    inside = cell < ROWS
    for p in range(2):
        solve_ref[ROWS * p : ROWS * (p + 1), :] = -1.0 / (waves[p] + both_ref[...])
        _, _, theta = decay(waves[p] + lam_col_ref[...])
        theta = jnp.concatenate([theta, theta], 1)
        whole = 1.0 / (1.0 - jnp.exp(-(2.0 * (ROWS + 1)) * theta))
        for side in range(2):
            step = jnp.where(inside, cell if side == 0 else ROWS - 1 - cell, 0).astype(F32)
            value = jnp.exp(-(step + 1.0) * theta) * (1.0 - jnp.exp(-2.0 * (ROWS - step) * theta)) * whole
            at = COLS * (2 * p + side)
            reach_ref[at : at + COLS, :] = jnp.where(inside, value, 0.0)
    row = ids((8, COLS), 0)
    rho, gap, theta = decay(jnp.where(row >= 6, waves[1], waves[0]) + lam_row_ref[...])
    period = 1.0 - jnp.exp(-2.0 * NY * theta)
    chain_ref[0] = rho
    chain_ref[1] = jnp.exp(-1.0 * ROWS * theta)
    chain_ref[2] = jnp.exp(-1.0 * (ROWS + 1) * theta)
    chain_ref[3] = jnp.where(row >= 4, 1.0 / (gap * period), 0.0)
    chain_ref[4] = period
    shape = (24, COLS)
    row, lane = ids(shape, 0), ids(shape, 1)
    place = row % 6
    second = jnp.logical_or(place // 2 == 1, jnp.logical_and(place >= 4, lane >= 64))
    mu = mu_lane_ref[pl.ds(pl.multiple_of(24 * wall, 8), 24), :]
    rho, gap, theta = decay(jnp.where(second, waves[1], waves[0]) + mu)
    scale = 1.0 / (gap * (1.0 - jnp.exp(-1.0 * NZ * theta)))
    cross = jnp.exp(-(COLS + 1.0) * theta)
    step = -1.0 * COLS * theta
    first = place % 2 == 0

    def reach(n):
        return jnp.exp(step * lax.bitwise_and(n, STRIPS - 1).astype(F32))

    for group in range(16):
        other = 4 * group + row // 6
        rows = slice(24 * group, 24 * (group + 1))
        coming, own = reach(strip - 1 - other), rho * reach(other - strip)
        left_ref[rows, :] = scale * jnp.where(first, cross * coming + own, coming + cross * own)
        own, coming = rho * reach(strip - other), reach(other - strip - 1)
        right_ref[rows, :] = scale * jnp.where(first, cross * own + coming, own + cross * coming)
    for copy in copies:
        copy.wait()
    for p in range(2):
        rows = slice(ROWS * p, ROWS * (p + 1))
        cauchy_ref[rows, :] = 1.0 / (mu_ref[...] + (waves[p] + lam_row_ref[0:1, :]))


def strip_kernel(in_ref, chain_ref, reach_ref, ends_ref, fold_ref, mine_ref, out_ref, own_ref, lows_ref, highs_ref):
    wall = lax.axis_index("wall")
    rho, block, cross, scale, period = (chain_ref[i] for i in range(5))
    up, down = [], []
    for w in range(WALLS):
        first, last = in_ref[8 * w : 8 * w + 8, 0:COLS], in_ref[8 * w : 8 * w + 8, COLS : 2 * COLS]
        up.append(last + cross * first)
        down.append(first + cross * last)
    seq = up + down[::-1]
    carry = seq[0]
    for i in range(1, 2 * WALLS):
        carry = carry * block + seq[i]
    sums = [carry]
    for i in range(2 * WALLS - 1):
        sums.append(block * sums[-1] + seq[i] * period)
    sums.append(sums[0])
    row = ids((8, COLS), 0)
    ends = ends_ref[...]
    parts = []
    for w in range(WALLS):
        low = scale * (sums[w] + rho * sums[2 * WALLS - w])
        high = scale * (rho * sums[w + 1] + sums[2 * WALLS - 1 - w])
        lows_ref[8 * w : 8 * w + 8, :] = low
        highs_ref[8 * w : 8 * w + 8, :] = high
        low, high = low * ends, high * ends
        planes = [jnp.where(row < 6, t, 0.0) for t in (low, high)] + [jnp.where(row < 6, 0.0, t) for t in (low, high)]
        parts.append(jnp.concatenate(planes, 1))
    mine = pl.ds(pl.multiple_of(8 * wall, 8), 8)
    own_ref[...] = jnp.where(row % 2 == 0, lows_ref[mine, :], highs_ref[mine, :])
    added = dot(jnp.concatenate(parts, 0), reach_ref[...])
    lines = jnp.where(ids((64, 256), 0) % 8 < 4, in_ref[...], added)
    folded = dot(fold_ref[pl.ds(pl.multiple_of(16 * wall, 16), 16), :], lines)
    modes = dot(folded[0:8, :ROWS], mine_ref[:ROWS, :]) + dot(folded[8:16, :ROWS], mine_ref[ROWS:, :])
    modes = jnp.where(ids((4, ROWS), 1) < HALF, modes[0:4], modes[4:8])
    tail = modes[:, COLS:]
    six = jnp.concatenate([modes[:, :COLS], jnp.concatenate([tail[0:2], tail[2:4]], 1)], 0)
    out = jnp.concatenate([six] * 4, 0)
    for group in range(16):
        out_ref[24 * group : 24 * (group + 1), :] = out


def ring_kernel(in_ref, left_ref, right_ref, mine_ref, spread_ref, ghost_ref, cauchy_ref, ends_z_ref, out_ref):
    wall = lax.axis_index("wall")
    pairs = []
    for weight_ref in (left_ref, right_ref):
        total = in_ref[0:24, :] * weight_ref[0:24, :]
        for group in range(1, 16):
            rows = slice(24 * group, 24 * (group + 1))
            total = total + in_ref[rows, :] * weight_ref[rows, :]
        six = (total[0:6] + total[6:12]) + (total[12:18] + total[18:24])
        pairs.append([six[2 * i : 2 * i + 1] + six[2 * i + 1 : 2 * i + 2] for i in range(3)])
    lines = []
    for plane in range(2):
        for side in range(2):
            tail = pairs[side][2][:, 64 * plane : 64 * plane + 64]
            lines.append(jnp.concatenate([pairs[side][plane], tail], 1))
    four = jnp.concatenate(lines, 0)
    even = ids((4, ROWS), 1) < HALF
    eight = jnp.concatenate([jnp.where(even, four, 0.0), jnp.where(even, 0.0, four)], 0)
    cells = [dot(eight, mine_ref[ROWS * k : ROWS * (k + 1), :], ((1,), (1,))) for k in range(2)]
    back = dot(spread_ref[pl.ds(pl.multiple_of(64 * wall, 64), 64), :], jnp.concatenate(cells, 0))
    ghost = ghost_ref[wall]
    rims = []
    for plane in range(2):
        both = jnp.concatenate([ghost * lines[2 * plane], ghost * lines[2 * plane + 1]], 0)
        both = dot(both, cauchy_ref[ROWS * plane : ROWS * (plane + 1), :])
        rims.append(both[:64] * ends_z_ref[0:1, :] + both[64:] * ends_z_ref[1:2, :])
    rim = jnp.where(ids((64, COLS), 0) % 8 < 6, rims[0], rims[1])
    out_ref[:, :COLS] = back[:, :COLS] + rim
    out_ref[:, COLS:] = jnp.concatenate([back[:, COLS:], jnp.zeros((64, 256 - ROWS), F32)], 1)


def final_kernel(in_ref, own_ref, freq_ref, solve_ref, sine_y_ref, sine_z_ref, ends_y_ref, ends_z_ref, out_ref):
    total = in_ref[0:8, :]
    for w in range(1, WALLS):
        total = total + in_ref[8 * w : 8 * w + 8, :]
    sine_y, sine_z = sine_y_ref[...], sine_z_ref[...]
    sides = dot(total[:, :ROWS], sine_y)
    rims = total[:, :COLS] + own_ref[...]
    for plane in range(2):
        rows = slice(ROWS * plane, ROWS * (plane + 1))
        lhs = jnp.concatenate([ends_y_ref[0:2, :], sides[2 * plane : 2 * plane + 2], jnp.zeros((4, ROWS), F32)], 0)
        rhs = jnp.concatenate([rims[4 + 2 * plane : 6 + 2 * plane], ends_z_ref[0:2, :], jnp.zeros((4, COLS), F32)], 0)
        freq = (freq_ref[rows, :] - dot(lhs, rhs, ((0,), (0,)))) * solve_ref[rows, :]
        out_ref[plane] = dot(dot(sine_y, freq), sine_z)


SMEM = pl.BlockSpec(memory_space=pltpu.SMEM)
VMEM = pl.BlockSpec(memory_space=pltpu.VMEM)
ANY = pl.BlockSpec(memory_space=pl.ANY)


def call(kernel, shapes, specs, *operands, scratch=()):
    outs = [jax.ShapeDtypeStruct(s, F32) for s in shapes]
    return pl.pallas_call(
        kernel,
        out_shape=outs if len(outs) > 1 else outs[0],
        in_specs=specs,
        out_specs=[VMEM] * len(outs) if len(outs) > 1 else VMEM,
        scratch_shapes=list(scratch),
        compiler_params=pltpu.CompilerParams(vmem_limit_bytes=24 << 20),
    )(*operands)


def exchange(block, axes):
    return lax.all_to_all(block, axes, split_axis=0, concat_axis=0, tiled=True)


def on_device(velocity, wave_x):
    t = {key: jnp.asarray(value) for key, value in tables().items()}
    sent, freq = call(
        box_kernel, [(64, 256), (2 * ROWS, COLS)], [SMEM] + [VMEM] * 8,
        wave_x, velocity, t["both"], t["sine_y"], t["sine_z"], t["sine_wide"], t["ends_y"], t["ends_z"], t["edge_w"],
    )
    solve, reach, chain, cauchy, left, right, mine = call(
        factor_kernel,
        [(2 * ROWS, COLS), (4 * COLS, 256), (5, 8, COLS), (2 * ROWS, COLS), (384, COLS), (384, COLS), (2 * ROWS, ROWS)],
        [SMEM] + [VMEM] * 4 + [ANY] * 2,
        wave_x, t["both"], t["lam_col"], t["lam_row"], t["mu_lane"], t["mu_col"], t["cosine"],
        scratch=[pltpu.VMEM((ROWS, COLS), F32), pltpu.SemaphoreType.DMA((2,))],
    )
    sent = exchange(sent.reshape(8, 8, 256), "wall").reshape(64, 256)
    modes, own = call(
        strip_kernel, [(384, COLS), (8, COLS)], [VMEM] * 6,
        sent, chain, reach, t["ends_tile"], t["fold"], mine,
        scratch=[pltpu.VMEM((64, COLS), F32)] * 2,
    )
    modes = exchange(modes.reshape(192, 2, COLS), "span").reshape(384, COLS)
    back = call(
        ring_kernel, [(64, 256)], [VMEM] * 8,
        modes, left, right, mine, t["spread"], t["ghost"], cauchy, t["ends_z"],
    )
    back = exchange(back.reshape(8, 8, 256), "wall").reshape(64, 256)
    return call(
        final_kernel, [(2, ROWS, COLS)], [VMEM] * 8,
        back, own, freq, solve, t["sine_y"], t["sine_z"], t["ends_y"], t["ends_z"],
    )


def solution(mesh):
    placed = (P(None, None, "wall", "span"), P())
    return jax.shard_map(
        on_device, mesh=mesh, in_specs=placed, out_specs=P(None, "wall", "span"), check_vma=False
    )
```

profile of v0, /device:TPU:1, one launch (start us, length us, event | category | flops | bytes accessed | tf_op | source)
XLA Modules:
  0.0 71.5 jit_solution(13937501013520030709)
XLA Ops:
  0.0 0.0 copy-start.2
  0.0 0.9 %copy-done.2 = f32[192,192]{1,0:T(8,128)S(1)} copy-done((f32[192,192]{1,0:T(8,128)S(1)}, f32[192,192]{1,0:T(8,128)}, u32[]{:S(2)}) %copy-start.2) | copy-done | bytes 147480
  0.9 0.0 copy-start.4
  0.9 1.1 %copy-done.4 = f32[3,2,192,128]{3,2,1,0:T(8,128)S(1)} copy-done((f32[3,2,192,128]{3,2,1,0:T(8,128)S(1)}, f32[3,2,192,128]{3,2,1,0:T(8,128)}, u32[]{:S(2)}) %copy-start.4) | copy-done | bytes 589848
  2.0 0.0 copy-start.6
  2.0 0.9 %copy-done.6 = f32[192,128]{1,0:T(8,128)S(1)} copy-done((f32[192,128]{1,0:T(8,128)S(1)}, f32[192,128]{1,0:T(8,128)}, u32[]{:S(2)}) %copy-start.6) | copy-done | bytes 98328
  2.9 0.0 copy-start.8
  2.9 0.8 %copy-done.8 = f32[128,128]{1,0:T(8,128)S(1)} copy-done((f32[128,128]{1,0:T(8,128)S(1)}, f32[128,128]{1,0:T(8,128)}, u32[]{:S(2)}) %copy-start.8) | copy-done | bytes 65560
  3.7 0.0 copy-start.11
  3.7 0.9 %copy-done.11 = f32[192,256]{1,0:T(8,128)S(1)} copy-done((f32[192,256]{1,0:T(8,128)S(1)}, f32[192,256]{1,0:T(8,128)}, u32[]{:S(2)}) %copy-start.11) | copy-done | bytes 196632
  4.7 0.0 copy-start.15
  4.7 0.7 copy-done.15
  5.3 0.0 copy-start.17
  5.3 0.7 copy-done.17
  6.0 0.0 copy-start.21
  6.0 0.7 copy-done.21
  6.7 0.0 copy-start.22
  6.7 0.7 copy-done.22
  7.4 0.0 copy-start.14
  7.4 0.0 copy-start.19
  7.4 0.0 copy-start.5
  7.4 0.0 copy-start.10
  7.4 3.9 %shard_map.172 = (f32[64,256]{1,0:T(8,128)}, f32[384,128]{1,0:T(8,128)S(1)}) custom-call(f32[2]{0:T(128)S(1)} %copy-done.22, f32[3,2,192,128]{3,2,1,0:T(8,128)S(1)} %copy-done.4, f32[192,128]{1,0:T(8,128)S(1)} %copy-done.6, f32[192,192]{1,0:T(8,128)S(1)} %copy-done.2, f32[128,128]{1,0:T(8,128)S(1)} %copy-done.8, f32[192,256]{1,0:T(8,128)S(1)} %copy-done.11, ...), custom_call_target="tpu_custom_call" | custom-call | tf_op jit(solution)/shard_map/pallas_call | solution.py:277
  11.3 0.0 copy-start.16
  11.3 7.8 %all-to-all-start = ((f32[8,8,256]{2,1,0:T(8,128)}), f32[8,8,256]{2,1,0:T(8,128)S(1)}, u32[]{:S(2)}, u32[]{:S(2)}) async-start(f32[8,8,256]{2,1,0:T(8,128)} %bitcast), calls=%async_computation | async-start | bytes 131072 | tf_op jit(solution)/shard_map/all_to_all | solution.py:288
  19.0 0.0 copy-start
  19.0 1.9 %copy-done = f32[8,384,192]{2,1,0:T(8,128)S(1)} copy-done((f32[8,384,192]{2,1,0:T(8,128)S(1)}, f32[8,384,192]{2,1,0:T(8,128)}, u32[]{:S(2)}) %copy-start) | copy-done | bytes 2359320
  20.9 0.0 copy-start.1
  20.9 1.1 %copy-done.1 = f32[8,192,128]{2,1,0:T(8,128)S(1)} copy-done((f32[8,192,128]{2,1,0:T(8,128)S(1)}, f32[8,192,128]{2,1,0:T(8,128)}, u32[]{:S(2)}) %copy-start.1) | copy-done | bytes 786456
  22.1 0.0 copy-start.7
  22.1 0.9 %copy-done.7 = f32[192,128]{1,0:T(8,128)S(1)} copy-done((f32[192,128]{1,0:T(8,128)S(1)}, f32[192,128]{1,0:T(8,128)}, u32[]{:S(2)}) %copy-start.7) | copy-done | bytes 98328
  23.0 0.0 copy-start.12
  23.0 0.9 %copy-done.12 = f32[192,128]{1,0:T(8,128)S(1)} copy-done((f32[192,128]{1,0:T(8,128)S(1)}, f32[192,128]{1,0:T(8,128)}, u32[]{:S(2)}) %copy-start.12) | copy-done | bytes 98328
  23.8 0.0 copy-start.13
  23.8 0.8 %copy-done.13 = f32[128,128]{1,0:T(8,128)S(1)} copy-done((f32[128,128]{1,0:T(8,128)S(1)}, f32[128,128]{1,0:T(8,128)}, u32[]{:S(2)}) %copy-start.13) | copy-done | bytes 65560
  24.7 0.0 copy-start.20
  24.7 0.7 copy-done.20
  25.4 0.0 copy-start.23
  25.4 0.7 copy-done.23
  26.0 0.0 copy-start.3
  26.0 0.0 copy-start.9
  26.0 0.0 copy-start.18
  26.0 1.5 %shard_map.173 = (f32[384,128]{1,0:T(8,128)S(1)}, f32[512,256]{1,0:T(8,128)S(1)}, f32[5,8,128]{2,1,0:T(8,128)S(1)}, f32[384,128]{1,0:T(8,128)S(1)}, f32[384,128]...) custom-call(f32[2]{0:T(128)S(1)} %copy-done.23, f32[192,128]{1,0:T(8,128)S(1)} %copy-done.7, ...), custom_call_target="tpu_custom_call" | custom-call | tf_op jit(solution)/shard_map/pallas_call | solution.py:277
  27.6 0.0 all-to-all-done
  27.6 0.0 copy-done.14
  27.6 0.0 copy-done.19
  27.6 1.3 %shard_map.174 = (f32[384,128]{1,0:T(8,128)S(1)}, f32[8,128]{1,0:T(8,128)S(1)}) custom-call(f32[64,256]{1,0:T(8,128)S(1)} %bitcast.8, f32[5,8,128]{2,1,0:T(8,128)S(1)} %get-tuple-element.17.chain_ref, f32[512,256]{1,0:T(8,128)S(1)} %get-tuple-element.18.reach_ref, f32[8,128]{1,0:T(8,128)S(1)} %copy-done.19, f32[128,64]{1,0:T(8,128)S(1)} %copy-done.14, ...), custom_call_target="tpu_custom_call" | custom-call | tf_op jit(solution)/shard_map/pallas_call | solution.py:277
  28.9 25.0 %all_to_all.15 = f32[192,2,128]{2,1,0:T(2,128)S(1)} all-to-all(f32[192,2,128]{2,1,0:T(2,128)S(1)} %bitcast.10), channel_id=1, replica_groups=mesh['span'=64,'wall'=8] {'span'}, dimensions={0} | all-to-all | bytes 393216 | tf_op jit(solution)/shard_map/all_to_all | solution.py:288
  53.9 0.0 copy-done.5
  53.9 0.0 copy-done.10
  53.9 0.0 copy-done.16
  53.9 1.0 %shard_map.175 = f32[64,256]{1,0:T(8,128)S(1)} custom-call(f32[384,128]{1,0:T(8,128)S(1)} %bitcast.6, f32[384,128]{1,0:T(8,128)S(1)} %get-tuple-element.21.left_ref, f32[384,128]{1,0:T(8,128)S(1)} %get-tuple-element.22.right_ref, f32[384,192]{1,0:T(8,128)S(1)} %get-tuple-element.19.mine_ref, f32[512,16]{1,0:T(8,128)S(1)} %copy-done.10, ...), custom_call_target="tpu_custom_call" | custom-call | tf_op jit(solution)/shard_map/pallas_call | solution.py:277
  54.9 13.9 %all_to_all.16 = f32[8,8,256]{2,1,0:T(8,128)S(1)} all-to-all(f32[8,8,256]{2,1,0:T(8,128)S(1)} %bitcast.9), channel_id=1, replica_groups=mesh['span'=64,'wall'=8] {'wall'}, dimensions={0} | all-to-all | bytes 131072 | tf_op jit(solution)/shard_map/all_to_all | solution.py:288
  68.8 0.0 copy-done.3
  68.8 0.0 copy-done.9
  68.8 0.0 copy-done.18
  68.8 2.7 %shard_map.176 = f32[2,192,128]{2,1,0:T(8,128)} custom-call(f32[64,256]{1,0:T(8,128)S(1)} %bitcast.7, f32[8,128]{1,0:T(8,128)S(1)} %get-tuple-element.24.own_ref, f32[384,128]{1,0:T(8,128)S(1)} %get-tuple-element.25.freq_ref, f32[384,128]{1,0:T(8,128)S(1)} %get-tuple-element.26.solve_ref, f32[192,192]{1,0:T(8,128)S(1)} %copy-done.3, ...), custom_call_target="tpu_custom_call" | custom-call | tf_op jit(solution)/shard_map/pallas_call | solution.py:277
Async XLA Ops:
  0.0 0.9 %copy-start.2 = (f32[192,192]{1,0:T(8,128)S(1)}, f32[192,192]{1,0:T(8,128)}, u32[]{:S(2)}) copy-start(f32[192,192]{1,0:T(8,128)} %constant.32.clone.sine_y_ref) | copy-start | bytes 442372
  0.9 1.1 %copy-start.4 = (f32[3,2,192,128]{3,2,1,0:T(8,128)S(1)}, f32[3,2,192,128]{3,2,1,0:T(8,128)}, u32[]{:S(2)}) copy-start(f32[3,2,192,128]{3,2,1,0:T(8,128)} %vel_ref.1) | copy-start | bytes 1769476
  2.0 0.9 %copy-start.6 = (f32[192,128]{1,0:T(8,128)S(1)}, f32[192,128]{1,0:T(8,128)}, u32[]{:S(2)}) copy-start(f32[192,128]{1,0:T(8,128)} %constant.39.clone.both_ref) | copy-start | bytes 294916
  2.9 0.8 %copy-start.8 = (f32[128,128]{1,0:T(8,128)S(1)}, f32[128,128]{1,0:T(8,128)}, u32[]{:S(2)}) copy-start(f32[128,128]{1,0:T(8,128)} %constant.33.clone.sine_z_ref) | copy-start | bytes 196612
  3.7 0.9 %copy-start.11 = (f32[192,256]{1,0:T(8,128)S(1)}, f32[192,256]{1,0:T(8,128)}, u32[]{:S(2)}) copy-start(f32[192,256]{1,0:T(8,128)} %constant.34.clone.wide_ref) | copy-start | bytes 589828
  4.7 0.7 copy-start.15
  5.3 0.7 copy-start.17
  6.0 0.7 copy-start.21
  6.7 0.7 copy-start.22
  7.4 20.2 %copy-start.14 = (f32[128,64]{1,0:T(8,128)S(1)}, f32[128,64]{1,0:T(8,128)}, u32[]{:S(2)}) copy-start(f32[128,64]{1,0:T(8,128)} %constant.43.clone.fold_ref) | copy-start | bytes 98308
  7.4 20.2 %copy-start.19 = (f32[8,128]{1,0:T(8,128)S(1)}, f32[8,128]{1,0:T(8,128)}, u32[]{:S(2)}) copy-start(f32[8,128]{1,0:T(8,128)} %constant.38.clone.ends_ref) | copy-start | bytes 12292
  7.4 46.5 %copy-start.5 = (f32[8,64,192]{2,1,0:T(8,128)S(1)}, f32[8,64,192]{2,1,0:T(8,128)}, u32[]{:S(2)}) copy-start(f32[8,64,192]{2,1,0:T(8,128)} %constant.45.clone.ghost_ref) | copy-start | bytes 1179652
  7.4 46.5 %copy-start.10 = (f32[512,16]{1,0:T(8,128)S(1)}, f32[512,16]{1,0:T(8,128)}, u32[]{:S(2)}) copy-start(f32[512,16]{1,0:T(8,128)} %constant.44.clone.spread_ref) | copy-start | bytes 98308
  11.3 42.7 %copy-start.16 = (f32[8,128]{1,0:T(8,128)S(1)}, f32[8,128]{1,0:T(8,128)}, u32[]{:S(2)}) copy-start(f32[8,128]{1,0:T(8,128)} %constant.36.clone.ends_z_ref) | copy-start | bytes 12292
  11.3 16.3 %all-to-all-start = ((f32[8,8,256]{2,1,0:T(8,128)}), f32[8,8,256]{2,1,0:T(8,128)S(1)}, u32[]{:S(2)}, u32[]{:S(2)}) async-start(f32[8,8,256]{2,1,0:T(8,128)} %bitcast), calls=%async_computation | async-start | bytes 131072 | tf_op jit(solution)/shard_map/all_to_all | solution.py:288
  19.0 1.9 %copy-start = (f32[8,384,192]{2,1,0:T(8,128)S(1)}, f32[8,384,192]{2,1,0:T(8,128)}, u32[]{:S(2)}) copy-start(f32[8,384,192]{2,1,0:T(8,128)} %constant.42.clone.cosine_ref) | copy-start | bytes 7077892
  20.9 1.1 %copy-start.1 = (f32[8,192,128]{2,1,0:T(8,128)S(1)}, f32[8,192,128]{2,1,0:T(8,128)}, u32[]{:S(2)}) copy-start(f32[8,192,128]{2,1,0:T(8,128)} %constant.46.clone.mu_col_ref) | copy-start | bytes 2359300
  22.1 0.9 %copy-start.7 = (f32[192,128]{1,0:T(8,128)S(1)}, f32[192,128]{1,0:T(8,128)}, u32[]{:S(2)}) copy-start(f32[192,128]{1,0:T(8,128)} %constant.39.clone.both_ref) | copy-start | bytes 294916
  23.0 0.9 %copy-start.12 = (f32[192,128]{1,0:T(8,128)S(1)}, f32[192,128]{1,0:T(8,128)}, u32[]{:S(2)}) copy-start(f32[192,128]{1,0:T(8,128)} %constant.47.clone.mu_lane_ref) | copy-start | bytes 294916
  23.8 0.8 %copy-start.13 = (f32[128,128]{1,0:T(8,128)S(1)}, f32[128,128]{1,0:T(8,128)}, u32[]{:S(2)}) copy-start(f32[128,128]{1,0:T(8,128)} %constant.40.clone.lam_col_ref) | copy-start | bytes 196612
  24.7 0.7 copy-start.20
  25.4 0.7 copy-start.23
  26.0 42.7 %copy-start.3 = (f32[192,192]{1,0:T(8,128)S(1)}, f32[192,192]{1,0:T(8,128)}, u32[]{:S(2)}) copy-start(f32[192,192]{1,0:T(8,128)} %constant.32.clone.sine_y_ref) | copy-start | bytes 442372
  26.0 42.7 %copy-start.9 = (f32[128,128]{1,0:T(8,128)S(1)}, f32[128,128]{1,0:T(8,128)}, u32[]{:S(2)}) copy-start(f32[128,128]{1,0:T(8,128)} %constant.33.clone.sine_z_ref) | copy-start | bytes 196612
  26.0 42.7 %copy-start.18 = (f32[8,192]{1,0:T(8,128)S(1)}, f32[8,192]{1,0:T(8,128)}, u32[]{:S(2)}) copy-start(f32[8,192]{1,0:T(8,128)} %constant.35.clone.ends_y_ref) | copy-start | bytes 18436
where the time goes:
time: 72.3 us; the launch traced here: 71.5 us
  blocking collectives  38.9 us (54%)
  local copies, waits for them, and re-layouts  14.4 us (20%)
  Pallas kernels  10.4 us (14%)
  starting transfers between devices  7.78 us (11%)
    all_to_all x2, blocking collectives, exchange(): return lax.all_to_all(block, axes, split_axis=0, concat_axis=0, tiled=True)  38.9 us
    unnamed x48, local copies, waits for them, and re-layouts  14.4 us
    pallas_call x5, Pallas kernels, call(): pl.pallas_call(kernel, out_shape=outs if len(outs) > 1 else outs[0], in_s...  10.4 us
    all_to_all x1, starting transfers between devices, exchange(): return lax.all_to_all(block, axes, split_axis=0, concat_axis=0, tiled=True)  7.78 us
  transfers between devices with their start and end apart: 1, of which 0 were waited for; matrix products, arithmetic and copies ran while one was open for 0% of the time, Pallas kernels for 2%

commit v1 on v0

v1 whole, which is shorter than its diff:
```python
import jax
import jax.numpy as jnp
import numpy as np
from jax import lax
from jax.experimental import pallas as pl
from jax.experimental.pallas import tpu as pltpu
from jax.sharding import PartitionSpec as P

F32 = jnp.float32
BF16 = jnp.bfloat16
EXACT = lax.Precision.HIGHEST
NY, NZ = 1536, 8192
WALLS, STRIPS = 8, 64
ROWS, COLS = NY // WALLS, NZ // STRIPS
HALF = ROWS // 2
SINE_Z, PICK, ENDS, BOX_ROWS = 384, 512, 768, 784
GHOST, WIDE_ROWS = 384, 448
SPREAD, FOLD, MU_LANE, NARROW_ROWS = 192, 256, 272, 296
LAM_ROW, ENDS_TILE, ENDS_Z, ENDS_Y, SHARED_ROWS = 128, 136, 144, 152, 168


def halves(table):
    high = table.astype(np.float32).astype(jnp.bfloat16).astype(np.float64)
    return high, table - high


def sine_table(n):
    i = np.arange(1, n + 1)
    return np.sqrt(2 / (n + 1)) * np.sin(np.pi * np.outer(i, i) / (n + 1)), 4 * np.sin(np.pi * i / (2 * (n + 1))) ** 2


def tables():
    sine_y, mu_box = sine_table(ROWS)
    sine_z, lam = sine_table(COLS)
    ends_tile = np.zeros((8, COLS))
    ends_tile[4] = ends_tile[6] = sine_z[0]
    ends_tile[5] = ends_tile[7] = sine_z[-1]
    r = np.arange(ROWS)
    wall = np.arange(WALLS)
    cosine = np.zeros((WALLS, 2 * ROWS, ROWS))
    fold = np.zeros((WALLS, 16, 64))
    spread = np.zeros((WALLS, 64, 16))
    ghost = np.zeros((WALLS, 64, ROWS))
    mu_col = np.zeros((WALLS, ROWS, COLS))
    mu_lane = np.zeros((WALLS, 24, COLS))
    for c in range(WALLS):
        mode = (c + 8 * np.arange(2)[:, None] + 16 * np.arange(HALF)[None, :]).reshape(-1)
        norm = np.where(mode == 0, np.sqrt(1 / NY), np.sqrt(2 / NY))
        angle = np.pi * np.outer(2 * r + 1, mode) / (2 * NY)
        cosine[c, :ROWS] = norm * np.cos(angle)
        cosine[c, ROWS:] = norm * np.sin(angle)
        for par in range(2):
            turn = np.pi * (c + 8 * par) * wall / 8
            for line in range(4):
                for w in range(WALLS):
                    for s in (line, line + 4):
                        fold[c, 4 * par + line, 8 * w + s] = np.cos(turn[w])
                        fold[c, 8 + 4 * par + line, 8 * w + s] = -np.sin(turn[w])
                    spread[c, 8 * w + line, 4 * par + line] = np.cos(turn[w])
                    spread[c, 8 * w + line, 8 + 4 * par + line] = -np.sin(turn[w])
        for w in range(WALLS):
            for g, y in enumerate((ROWS * w - 1, ROWS * (w + 1))):
                row = norm * np.cos(np.pi * mode * (2 * y + 1) / (2 * NY))
                ghost[c, 8 * w + 4 + g] = ghost[c, 8 * w + 6 + g] = row
        mu = 4 * np.sin(np.pi * mode / (2 * NY)) ** 2
        mu_col[c] = mu[:, None]
        six = np.stack([mu[:128]] * 4 + [np.concatenate([mu[128:], mu[128:]])] * 2)
        mu_lane[c] = np.concatenate([six] * 4)
    sine = np.zeros((2 * ROWS, 256))
    sine[:ROWS, :ROWS], sine[ROWS:, :ROWS] = halves(sine_y)
    pick = np.zeros((2 * COLS, COLS))
    for plane in range(2):
        pick[COLS * plane : COLS * (plane + 1), 2 * plane] = sine_z[0]
        pick[COLS * plane : COLS * (plane + 1), 2 * plane + 1] = sine_z[-1]
    ends = np.zeros((16, 256))
    ends[0:2, :ROWS], ends[8:10, :ROWS] = halves(sine_y[[0, -1]])
    boxes = np.concatenate([sine, np.concatenate(halves(sine_z), 1), np.concatenate(halves(pick), 1), ends])
    wide = np.zeros((WALLS, WIDE_ROWS, 256))
    wide[:, :GHOST, :ROWS], wide[:, GHOST:, :ROWS] = cosine, ghost
    narrow = np.zeros((WALLS, NARROW_ROWS, COLS))
    narrow[:, :SPREAD], narrow[:, SPREAD:FOLD, :16] = mu_col, spread
    narrow[:, FOLD:MU_LANE, :64], narrow[:, MU_LANE:] = fold, mu_lane
    ends_z = np.zeros((8, COLS))
    ends_z[0], ends_z[1] = sine_z[0], sine_z[-1]
    ends_y = np.zeros((8, 256))
    ends_y[0, :ROWS], ends_y[1, :ROWS] = sine_y[0], sine_y[-1]
    shared = np.concatenate([np.repeat(lam[:, None], COLS, 1), np.repeat(lam[None], 8, 0), ends_tile, ends_z, ends_y[:, :COLS], ends_y[:, COLS:]])
    both = mu_box[:, None] + lam[None, :]
    names = dict(both=both, wide=wide, narrow=narrow, shared=shared)
    return {key: np.asarray(value, np.float32) for key, value in names.items()}, np.asarray(boxes, np.float32)


def dot(a, b, dims=((1,), (0,))):
    return lax.dot_general(a, b, (dims, ((), ())), precision=EXACT, preferred_element_type=F32)


def ids(shape, dim):
    return lax.broadcasted_iota(jnp.int32, shape, dim)


def parts(value):
    high = value.astype(BF16).astype(F32)
    return [high.astype(BF16), (value - high).astype(BF16)]


def stacked(value):
    high = value.astype(BF16).astype(F32)
    return jnp.concatenate([high, value - high], 0).astype(BF16)


def joined(product, rows, at):
    here, beside = slice(at, at + COLS), slice(at + COLS, at + 2 * COLS)
    return product[:rows, here] + (product[:rows, beside] + product[rows:, here])


def fast(a, b):
    return jnp.dot(a, b, preferred_element_type=F32)


def box_kernel(
    wave_hbm, vel_hbm, both_hbm, boxes_hbm,
    out_ref, freq_ref, solve_ref, boxes_ref,
    wave_ref, vel_ref, both_ref, sems,
):
    pairs = [
        (wave_hbm, wave_ref), (both_hbm, both_ref),
        (vel_hbm.at[:, 0], vel_ref.at[:, 0]), (vel_hbm.at[:, 1], vel_ref.at[:, 1]), (boxes_hbm, boxes_ref),
    ]
    copies = [pltpu.make_async_copy(*pair, sems.at[i]) for i, pair in enumerate(pairs)]
    for copy in copies:
        copy.start()
    row, lane = ids((ROWS, COLS), 0), ids((ROWS, COLS), 1)
    wall = lax.axis_index("wall")
    low = jnp.where(wall > 0, -0.5, 0.0)
    high = jnp.where(wall < WALLS - 1, 0.5, 0.0)
    copies[0].wait()
    copies[1].wait()
    for plane in range(2):
        wave = wave_ref[plane]
        solve_ref[ROWS * plane : ROWS * (plane + 1), :] = -1.0 / (wave * wave + both_ref[...])
    sources, rims, halo = [], [], jnp.zeros((ROWS, COLS), F32)
    for plane in range(2):
        copies[2 + plane].wait()
        u, v, w = (vel_ref[c, plane] for c in range(3))
        above = jnp.where(row == ROWS - 1, 0.0, pltpu.roll(v, ROWS - 1, 0))
        below = jnp.where(row == 0, 0.0, pltpu.roll(v, 1, 0))
        after = jnp.where(lane == COLS - 1, 0.0, pltpu.roll(w, COLS - 1, 1))
        before = jnp.where(lane == 0, 0.0, pltpu.roll(w, 1, 1))
        sources += parts(wave_ref[plane] * u + 0.5 * ((above - below) + (after - before)))
        rims += [low * v[0:1], high * v[ROWS - 1 :]]
        for side in range(2):
            moved = pltpu.roll(w, 2 * plane + 2 * side, 1) if plane + side else w
            halo = jnp.where(lane == 2 * plane + side, (side - 0.5) * moved, halo)
    copies[4].wait()
    sine, sine_z = boxes_ref[:SINE_Z, :ROWS], boxes_ref[SINE_Z:PICK, :]
    product = fast(sine, jnp.concatenate(sources, 1))
    product = fast(jnp.concatenate([stacked(joined(product, ROWS, 256 * p)) for p in range(2)], 0), sine_z)
    insides = []
    for plane in range(2):
        freq = joined(product[2 * ROWS * plane : 2 * ROWS * (plane + 1)], ROWS, 0)
        rows = slice(ROWS * plane, ROWS * (plane + 1))
        freq_ref[rows, :] = freq
        insides.append(parts(freq * solve_ref[rows, :]))
    ends = fast(boxes_ref[ENDS:BOX_ROWS, :ROWS], jnp.concatenate(insides[0] + insides[1], 1))
    ends = [joined(ends, 8, 256 * p)[0:2] for p in range(2)]
    rims = fast(stacked(jnp.concatenate(rims + [jnp.zeros((4, COLS), F32)], 0)), sine_z)
    ends = jnp.concatenate(ends, 0) + joined(rims, 8, 0)[0:4]
    cols = jnp.concatenate([jnp.concatenate([insides[0][k], insides[1][k]], 1) for k in range(2)], 0)
    cols = joined(fast(cols, boxes_ref[PICK:ENDS, :]), ROWS, 0)
    cols = joined(fast(sine, jnp.concatenate(parts(cols), 1)), ROWS, 0) + halo
    edges = jnp.concatenate([cols, jnp.zeros((256 - ROWS, COLS), F32)], 0).T[0:4]
    tile = [jnp.concatenate([ends[i : i + 1], ends[i + 1 : i + 2]], 1) for i in (0, 0, 2, 2)]
    tile = jnp.concatenate([edges] + tile, 0)
    for w in range(WALLS):
        out_ref[8 * w : 8 * w + 8, :] = tile


def decay(shift):
    root = jnp.sqrt(shift * (shift + 4.0))
    delta = (shift + root) / (2.0 + shift + root)
    return 1.0 - delta, delta * (2.0 - delta), -jnp.log1p(-delta)


def factor_kernel(
    wave_hbm, wide_hbm, narrow_hbm, shared_hbm,
    reach_ref, chain_ref, cauchy_ref, left_ref, right_ref, wide_ref, narrow_ref, shared_ref,
    wave_ref, sems,
):
    strip, wall = lax.axis_index("span"), lax.axis_index("wall")
    pairs = [(wave_hbm, wave_ref), (shared_hbm, shared_ref), (narrow_hbm.at[wall], narrow_ref), (wide_hbm.at[wall], wide_ref)]
    copies = [pltpu.make_async_copy(*pair, sems.at[i]) for i, pair in enumerate(pairs)]
    for copy in copies:
        copy.start()
    for copy in copies[:3]:
        copy.wait()
    waves = [wave_ref[p] * wave_ref[p] for p in range(2)]
    cell = ids((COLS, 256), 1)
    inside = cell < ROWS
    for p in range(2):
        _, _, theta = decay(waves[p] + shared_ref[:LAM_ROW, :])
        theta = jnp.concatenate([theta, theta], 1)
        whole = 1.0 / (1.0 - jnp.exp(-(2.0 * (ROWS + 1)) * theta))
        for side in range(2):
            step = jnp.where(inside, cell if side == 0 else ROWS - 1 - cell, 0).astype(F32)
            value = jnp.exp(-(step + 1.0) * theta) * (1.0 - jnp.exp(-2.0 * (ROWS - step) * theta)) * whole
            at = COLS * (2 * p + side)
            reach_ref[at : at + COLS, :] = jnp.where(inside, value, 0.0)
    row = ids((8, COLS), 0)
    rho, gap, theta = decay(jnp.where(row >= 6, waves[1], waves[0]) + shared_ref[LAM_ROW:ENDS_TILE, :])
    period = 1.0 - jnp.exp(-2.0 * NY * theta)
    chain_ref[0] = rho
    chain_ref[1] = jnp.exp(-1.0 * ROWS * theta)
    chain_ref[2] = jnp.exp(-1.0 * (ROWS + 1) * theta)
    chain_ref[3] = jnp.where(row >= 4, 1.0 / (gap * period), 0.0)
    chain_ref[4] = period
    shape = (24, COLS)
    row, lane = ids(shape, 0), ids(shape, 1)
    place = row % 6
    second = jnp.logical_or(place // 2 == 1, jnp.logical_and(place >= 4, lane >= 64))
    rho, gap, theta = decay(jnp.where(second, waves[1], waves[0]) + narrow_ref[MU_LANE:, :])
    scale = 1.0 / (gap * (1.0 - jnp.exp(-1.0 * NZ * theta)))
    cross = jnp.exp(-(COLS + 1.0) * theta)
    step = -1.0 * COLS * theta
    first = place % 2 == 0

    def reach(n):
        return jnp.exp(step * lax.bitwise_and(n, STRIPS - 1).astype(F32))

    for group in range(16):
        other = 4 * group + row // 6
        rows = slice(24 * group, 24 * (group + 1))
        coming, own = reach(strip - 1 - other), rho * reach(other - strip)
        left_ref[rows, :] = scale * jnp.where(first, cross * coming + own, coming + cross * own)
        own, coming = rho * reach(strip - other), reach(other - strip - 1)
        right_ref[rows, :] = scale * jnp.where(first, cross * own + coming, own + cross * coming)
    for p in range(2):
        rows = slice(ROWS * p, ROWS * (p + 1))
        cauchy_ref[rows, :] = 1.0 / (narrow_ref[:SPREAD, :] + (waves[p] + shared_ref[LAM_ROW : LAM_ROW + 1, :]))
    copies[3].wait()


def strip_kernel(in_ref, chain_ref, reach_ref, wide_ref, narrow_ref, shared_ref, out_ref, own_ref, lows_ref, highs_ref):
    wall = lax.axis_index("wall")
    rho, block, cross, scale, period = (chain_ref[i] for i in range(5))
    up, down = [], []
    for w in range(WALLS):
        first, last = in_ref[8 * w : 8 * w + 8, 0:COLS], in_ref[8 * w : 8 * w + 8, COLS : 2 * COLS]
        up.append(last + cross * first)
        down.append(first + cross * last)
    seq = up + down[::-1]
    carry = seq[0]
    for i in range(1, 2 * WALLS):
        carry = carry * block + seq[i]
    sums = [carry]
    for i in range(2 * WALLS - 1):
        sums.append(block * sums[-1] + seq[i] * period)
    sums.append(sums[0])
    row = ids((8, COLS), 0)
    ends = shared_ref[ENDS_TILE:ENDS_Z, :]
    blocks = []
    for w in range(WALLS):
        low = scale * (sums[w] + rho * sums[2 * WALLS - w])
        high = scale * (rho * sums[w + 1] + sums[2 * WALLS - 1 - w])
        lows_ref[8 * w : 8 * w + 8, :] = low
        highs_ref[8 * w : 8 * w + 8, :] = high
        low, high = low * ends, high * ends
        planes = [jnp.where(row < 6, t, 0.0) for t in (low, high)] + [jnp.where(row < 6, 0.0, t) for t in (low, high)]
        blocks.append(jnp.concatenate(planes, 1))
    mine = pl.ds(pl.multiple_of(8 * wall, 8), 8)
    own_ref[...] = jnp.where(row % 2 == 0, lows_ref[mine, :], highs_ref[mine, :])
    added = dot(jnp.concatenate(blocks, 0), reach_ref[...])
    lines = jnp.where(ids((64, 256), 0) % 8 < 4, in_ref[...], added)
    folded = dot(narrow_ref[FOLD:MU_LANE, :64], lines)
    modes = dot(folded[0:8, :ROWS], wide_ref[:ROWS, :ROWS]) + dot(folded[8:16, :ROWS], wide_ref[ROWS:GHOST, :ROWS])
    modes = jnp.where(ids((4, ROWS), 1) < HALF, modes[0:4], modes[4:8])
    tail = modes[:, COLS:]
    six = jnp.concatenate([modes[:, :COLS], jnp.concatenate([tail[0:2], tail[2:4]], 1)], 0)
    out = jnp.concatenate([six] * 4, 0)
    for group in range(16):
        out_ref[24 * group : 24 * (group + 1), :] = out


def ring_kernel(in_ref, left_ref, right_ref, wide_ref, narrow_ref, cauchy_ref, shared_ref, out_ref):
    pairs = []
    for weight_ref in (left_ref, right_ref):
        total = in_ref[0:24, :] * weight_ref[0:24, :]
        for group in range(1, 16):
            rows = slice(24 * group, 24 * (group + 1))
            total = total + in_ref[rows, :] * weight_ref[rows, :]
        six = (total[0:6] + total[6:12]) + (total[12:18] + total[18:24])
        pairs.append([six[2 * i : 2 * i + 1] + six[2 * i + 1 : 2 * i + 2] for i in range(3)])
    lines = []
    for plane in range(2):
        for side in range(2):
            tail = pairs[side][2][:, 64 * plane : 64 * plane + 64]
            lines.append(jnp.concatenate([pairs[side][plane], tail], 1))
    four = jnp.concatenate(lines, 0)
    even = ids((4, ROWS), 1) < HALF
    eight = jnp.concatenate([jnp.where(even, four, 0.0), jnp.where(even, 0.0, four)], 0)
    cells = [dot(eight, wide_ref[ROWS * k : ROWS * (k + 1), :ROWS], ((1,), (1,))) for k in range(2)]
    back = dot(narrow_ref[SPREAD:FOLD, :16], jnp.concatenate(cells, 0))
    ghost = wide_ref[GHOST:, :ROWS]
    ends = shared_ref[ENDS_Z : ENDS_Z + 2, :]
    rims = []
    for plane in range(2):
        both = jnp.concatenate([ghost * lines[2 * plane], ghost * lines[2 * plane + 1]], 0)
        both = dot(both, cauchy_ref[ROWS * plane : ROWS * (plane + 1), :])
        rims.append(both[:64] * ends[0:1] + both[64:] * ends[1:2])
    rim = jnp.where(ids((64, COLS), 0) % 8 < 6, rims[0], rims[1])
    out_ref[:, :COLS] = back[:, :COLS] + rim
    out_ref[:, COLS:] = jnp.concatenate([back[:, COLS:], jnp.zeros((64, 256 - ROWS), F32)], 1)


def final_kernel(in_ref, own_ref, freq_ref, solve_ref, boxes_ref, shared_ref, out_ref):
    total = in_ref[0:8, :]
    for w in range(1, WALLS):
        total = total + in_ref[8 * w : 8 * w + 8, :]
    sine, sine_z = boxes_ref[:SINE_Z, :ROWS], boxes_ref[SINE_Z:PICK, :]
    both = stacked(total[:, :ROWS])
    sides = fast(both, boxes_ref[:ROWS, :])
    sides = sides[0:8] + (sides[8:16] + fast(both, boxes_ref[ROWS:SINE_Z, :])[0:8])
    rims = total[:, :COLS] + own_ref[...]
    ends_y = jnp.concatenate([shared_ref[ENDS_Y : ENDS_Y + 2, :], shared_ref[ENDS_Y + 8 : ENDS_Y + 10, :]], 1)
    freqs = []
    for plane in range(2):
        rows = slice(ROWS * plane, ROWS * (plane + 1))
        lhs = jnp.concatenate([ends_y, sides[2 * plane : 2 * plane + 2], jnp.zeros((4, 256), F32)], 0)[:, :ROWS]
        rhs = jnp.concatenate([rims[4 + 2 * plane : 6 + 2 * plane], shared_ref[ENDS_Z : ENDS_Z + 2, :], jnp.zeros((4, COLS), F32)], 0)
        freqs.append(stacked((freq_ref[rows, :] - dot(lhs, rhs, ((0,), (0,)))) * solve_ref[rows, :]))
    product = fast(jnp.concatenate(freqs, 0), sine_z)
    lines = [parts(joined(product[2 * ROWS * p : 2 * ROWS * (p + 1)], ROWS, 0)) for p in range(2)]
    product = fast(sine, jnp.concatenate(lines[0] + lines[1], 1))
    for plane in range(2):
        out_ref[plane] = joined(product, ROWS, 256 * plane)


SMEM = pl.BlockSpec(memory_space=pltpu.SMEM)
VMEM = pl.BlockSpec(memory_space=pltpu.VMEM)
HBM = pl.BlockSpec(memory_space=pltpu.HBM)


def call(kernel, shapes, specs, *operands, scratch=()):
    outs = [s if isinstance(s, jax.ShapeDtypeStruct) else jax.ShapeDtypeStruct(s, F32) for s in shapes]
    return pl.pallas_call(
        kernel,
        out_shape=outs if len(outs) > 1 else outs[0],
        in_specs=specs,
        out_specs=[VMEM] * len(outs) if len(outs) > 1 else VMEM,
        scratch_shapes=list(scratch),
        compiler_params=pltpu.CompilerParams(vmem_limit_bytes=24 << 20),
    )(*(pltpu.with_memory_space_constraint(x, pltpu.HBM) if s is HBM else x for s, x in zip(specs, operands)))


def exchange(block, axes):
    return lax.all_to_all(block, axes, split_axis=0, concat_axis=0, tiled=True)


def on_device(velocity, wave_x):
    names, boxes = tables()
    t = {key: jnp.asarray(value) for key, value in names.items()}
    sent, freq, solve, boxes = call(
        box_kernel,
        [(64, 256), (2 * ROWS, COLS), (2 * ROWS, COLS), jax.ShapeDtypeStruct((BOX_ROWS, 256), BF16)],
        [HBM] * 4, wave_x, velocity, t["both"], jnp.asarray(boxes, BF16),
        scratch=[
            pltpu.SMEM((2,), F32), pltpu.VMEM((3, 2, ROWS, COLS), F32), pltpu.VMEM((ROWS, COLS), F32),
            pltpu.SemaphoreType.DMA((5,)),
        ],
    )
    reach, chain, cauchy, left, right, wide, narrow, shared = call(
        factor_kernel,
        [
            (4 * COLS, 256), (5, 8, COLS), (2 * ROWS, COLS), (384, COLS), (384, COLS),
            (WIDE_ROWS, 256), (NARROW_ROWS, COLS), (SHARED_ROWS, COLS),
        ],
        [HBM] * 4, wave_x, t["wide"], t["narrow"], t["shared"],
        scratch=[pltpu.SMEM((2,), F32), pltpu.SemaphoreType.DMA((4,))],
    )
    sent = exchange(sent.reshape(8, 8, 256), "wall").reshape(64, 256)
    modes, own = call(
        strip_kernel, [(384, COLS), (8, COLS)], [VMEM] * 6,
        sent, chain, reach, wide, narrow, shared,
        scratch=[pltpu.VMEM((64, COLS), F32)] * 2,
    )
    modes = exchange(modes.reshape(192, 2, COLS), "span").reshape(384, COLS)
    back = call(ring_kernel, [(64, 256)], [VMEM] * 7, modes, left, right, wide, narrow, cauchy, shared)
    back = exchange(back.reshape(8, 8, 256), "wall").reshape(64, 256)
    return call(final_kernel, [(2, ROWS, COLS)], [VMEM] * 6, back, own, freq, solve, boxes, shared)


def solution(mesh):
    placed = (P(None, None, "wall", "span"), P())
    return jax.shard_map(
        on_device, mesh=mesh, in_specs=placed, out_specs=P(None, "wall", "span"), check_vma=False
    )
```

time: 72.3 us -> 57.9 us (0.80)
  local copies, waits for them, and re-layouts: 14.4 us -> 0 us
  waiting for transfers between devices: 0.01 us -> 5.61 us
  blocking collectives: 38.9 us -> 35.7 us
  Pallas kernels: 10.4 us -> 8.65 us
    unnamed x48 -> x0, local copies, waits for them, and re-layouts: 14.4 us -> none
    all_to_all x1, waiting for transfers between devices: 0.01 us -> 5.61 us  [exchange(): return lax.all_to_all(block, axes, split_axis=0, concat_axis=0, tiled=True)]
    all_to_all x2, blocking collectives: 38.9 us -> 35.7 us  [exchange(): return lax.all_to_all(block, axes, split_axis=0, concat_axis=0, tiled=True)]
    pallas_call x5, Pallas kernels: 10.4 us -> 8.65 us  [call(): pl.pallas_call(kernel, out_shape=outs if len(outs) > 1 else outs[0], in_s...]
  transfers between devices with their start and end apart: 1 -> 1, of which waited for: 0 -> 1; matrix products, arithmetic and copies ran while one was open for 0% -> 0% of each run, Pallas kernels for 2% -> 3%
where the time goes in v1:
time: 57.9 us; the launch traced here: 57.6 us
  blocking collectives  35.7 us (62%)
  Pallas kernels  8.65 us (15%)
  starting transfers between devices  7.66 us (13%)
  waiting for transfers between devices  5.61 us (10%)
    all_to_all x2, blocking collectives, exchange(): return lax.all_to_all(block, axes, split_axis=0, concat_axis=0, tiled=True)  35.7 us
    pallas_call x5, Pallas kernels, call(): pl.pallas_call(kernel, out_shape=outs if len(outs) > 1 else outs[0], in_s...  8.65 us
    all_to_all x1, starting transfers between devices, exchange(): return lax.all_to_all(block, axes, split_axis=0, concat_axis=0, tiled=True)  7.66 us
    all_to_all x1, waiting for transfers between devices, exchange(): return lax.all_to_all(block, axes, split_axis=0, concat_axis=0, tiled=True)  5.61 us
  transfers between devices with their start and end apart: 1, of which 1 were waited for; matrix products, arithmetic and copies ran while one was open for 0% of the time, Pallas kernels for 3%

profile of v1, /device:TPU:1, one launch (start us, length us, event | category | flops | bytes accessed | tf_op | source)
XLA Modules:
  0.0 57.6 jit_solution(15698750483900923007)
XLA Ops:
  0.0 3.1 %shard_map.73 = (f32[64,256]{1,0:T(8,128)}, f32[384,128]{1,0:T(8,128)S(1)}, f32[384,128]{1,0:T(8,128)S(1)}, bf16[784,256]{1,0:T(8,128)(2,1)S(1)}) custom-call(f32[2]{0:T(128)} %wave_hbm.3, f32[3,2,192,128]{3,2,1,0:T(8,128)} %vel_hbm.1, f32[192,128]{1,0:T(8,128)} %constant.10.clone.both_hbm, bf16[784,256]{1,0:T(8,128)(2,1)} %constant.14.clone.boxes_hbm), custom_call_target="tpu_custom_call" | custom-call | tf_op jit(solution)/shard_map/pallas_call | solution.py:344
  3.1 7.7 %all-to-all-start = ((f32[8,8,256]{2,1,0:T(8,128)}), f32[8,8,256]{2,1,0:T(8,128)S(1)}, u32[]{:S(2)}, u32[]{:S(2)}) async-start(f32[8,8,256]{2,1,0:T(8,128)} %bitcast), calls=%async_computation | async-start | bytes 131072 | tf_op jit(solution)/shard_map/all_to_all | solution.py:355
  10.8 1.6 %shard_map.74 = (f32[512,256]{1,0:T(8,128)S(1)}, f32[5,8,128]{2,1,0:T(8,128)S(1)}, f32[384,128]{1,0:T(8,128)S(1)}, f32[384,128]{1,0:T(8,128)S(1)}, f32[384,128]{...) custom-call(f32[2]{0:T(128)} %wave_hbm.3, ...), custom_call_target="tpu_custom_call" | custom-call | tf_op jit(solution)/shard_map/pallas_call | solution.py:344
  12.4 5.6 %all-to-all-done = f32[8,8,256]{2,1,0:T(8,128)S(1)} async-done(((f32[8,8,256]{2,1,0:T(8,128)}), f32[8,8,256]{2,1,0:T(8,128)S(1)}, u32[]{:S(2)}, u32[]{:S(2)}) %all-to-all-start) | async-done | bytes 65568 | tf_op jit(solution)/shard_map/all_to_all | solution.py:355
  18.0 1.3 %shard_map.75 = (f32[384,128]{1,0:T(8,128)S(1)}, f32[8,128]{1,0:T(8,128)S(1)}) custom-call(f32[64,256]{1,0:T(8,128)S(1)} %bitcast.7, f32[5,8,128]{2,1,0:T(8,128)S(1)} %get-tuple-element.20.chain_ref, f32[512,256]{1,0:T(8,128)S(1)} %get-tuple-element.21.reach_ref, f32[448,256]{1,0:T(8,128)S(1)} %get-tuple-element.22.wide_ref, ...), custom_call_target="tpu_custom_call" | custom-call | tf_op jit(solution)/shard_map/pallas_call | solution.py:344
  19.3 26.2 %all_to_all.15 = f32[192,2,128]{2,1,0:T(2,128)S(1)} all-to-all(f32[192,2,128]{2,1,0:T(2,128)S(1)} %bitcast.10), channel_id=1, replica_groups=mesh['span'=64,'wall'=8] {'span'}, dimensions={0} | all-to-all | bytes 393216 | tf_op jit(solution)/shard_map/all_to_all | solution.py:355
  45.4 1.0 %shard_map.76 = f32[64,256]{1,0:T(8,128)S(1)} custom-call(f32[384,128]{1,0:T(8,128)S(1)} %bitcast.6, f32[384,128]{1,0:T(8,128)S(1)} %get-tuple-element.26.left_ref, f32[384,128]{1,0:T(8,128)S(1)} %get-tuple-element.27.right_ref, f32[448,256]{1,0:T(8,128)S(1)} %get-tuple-element.22.wide_ref, f32[296,128]{1,0:T(8,128)S(1)} %get-tuple-element.23.narrow_ref, ...), custom_call_target="tpu_custom_call" | custom-call | tf_op jit(solution)/shard_map/pallas_call | solution.py:344
  46.4 9.5 %all_to_all.16 = f32[8,8,256]{2,1,0:T(8,128)S(1)} all-to-all(f32[8,8,256]{2,1,0:T(8,128)S(1)} %bitcast.9), channel_id=1, replica_groups=mesh['span'=64,'wall'=8] {'wall'}, dimensions={0} | all-to-all | bytes 131072 | tf_op jit(solution)/shard_map/all_to_all | solution.py:355
  55.9 1.7 %shard_map.77 = f32[2,192,128]{2,1,0:T(8,128)} custom-call(f32[64,256]{1,0:T(8,128)S(1)} %bitcast.8, f32[8,128]{1,0:T(8,128)S(1)} %get-tuple-element.29.own_ref, f32[384,128]{1,0:T(8,128)S(1)} %get-tuple-element.30.freq_ref, f32[384,128]{1,0:T(8,128)S(1)} %get-tuple-element.31.solve_ref, bf16[784,256]{1,0:T(8,128)(2,1)S(1)} %get-tuple-element.32.boxes_ref, ...), custom_call_target="tpu_custom_call" | custom-call | tf_op jit(solution)/shard_map/pallas_call | solution.py:344
Async XLA Ops:
  3.1 14.9 %all-to-all-start = ((f32[8,8,256]{2,1,0:T(8,128)}), f32[8,8,256]{2,1,0:T(8,128)S(1)}, u32[]{:S(2)}, u32[]{:S(2)}) async-start(f32[8,8,256]{2,1,0:T(8,128)} %bitcast), calls=%async_computation | async-start | bytes 131072 | tf_op jit(solution)/shard_map/all_to_all | solution.py:355
